TPU v7x, 512 devices: a whole 4x4x16 slice. The times are simulated.
512 devices in a mesh: dp: 16 (over y, x), expert: 32 (over z, core).
Axes of the slice: x: 4, y: 4, z: 16, core: 2. Of those that a mesh axis runs over, the one named last changes fastest.
Arguments:
- inputs: bfloat16 [2048, 6144], P('expert', 'dp'), may hold values from -6 to 6
- grad_out: bfloat16 [2048, 6144], P('expert', 'dp'), may hold values from -6 to 6
- expert_ids: int32 [2048, 2], P('expert'), may hold values from 0 to 3, as said below
- live_counts: int32 [32], P('expert'), may hold values from 32 to 64, as said below
- router_weight: bfloat16 [6144, 4], P('dp'), may hold values from -0.078125 to 0.078125
- up_weight: bfloat16 [6144, 32768], P('dp', 'expert'), may hold values from -0.078125 to 0.078125
- down_weight: bfloat16 [6144, 32768], P('dp', 'expert'), may hold values from -0.0625 to 0.0625
Outputs:
- grad_inputs: bfloat16 [2048, 6144], P('expert', 'dp')
- grad_up: bfloat16 [6144, 32768], P('dp', 'expert')
- grad_down: bfloat16 [6144, 32768], P('dp', 'expert')
- grad_router: float32 [6144, 4], P('dp')
Inputs may be any that keep to these rules, and one draw needn't show every extreme that they name: `expert_ids`: each row names two different experts. Among the first live_counts[g] tokens of group g, each expert is named at most 32 times; one expert is named exactly 32 times in every group. `live_counts`: some group has all its slots live.
All inputs are finite; a program needn't handle non-finite values.
Results may differ from a plain program's by a relative error of at most 0.035.
Values may be sent and summed in bfloat16 or wider, within the bound.
A program may use at most 64 MiB of HBM per device.

v0:
```python
import jax
import jax.numpy as jnp
from jax import lax
from jax.sharding import PartitionSpec as P

ROOT_HALF = 0.7071067811865476
INV_ROOT_TWO_PI = 0.3989422804014327


def gelu_value(value):
    return 0.5 * value * (1.0 + jax.scipy.special.erf(value * ROOT_HALF))


def gelu_slope(value):
    return (
        0.5 * (1.0 + jax.scipy.special.erf(value * ROOT_HALF))
        + value * jnp.exp(-0.5 * value * value) * INV_ROOT_TWO_PI
    )


def activate(before_act, back_act, gate_column):
    active = gelu_value(before_act)
    hidden = lax.optimization_barrier(active.astype(jnp.bfloat16))
    gate_sum = jnp.sum(hidden.astype(jnp.float32) * back_act, axis=1)
    inner_grad = (gate_column * back_act * gelu_slope(before_act)).astype(jnp.bfloat16)
    weighted = (gate_column * active).astype(jnp.bfloat16)
    return (gate_sum, inner_grad, weighted)


def local(inputs, grad_out, expert_ids, live_counts, router_weight, up_weight, down_weight):
    per_group = inputs.shape[0]
    share = inputs.shape[1]
    experts = router_weight.shape[1]
    groups = lax.axis_size("expert")
    column_parts = groups // experts
    capacity = 2 * per_group // experts
    partial_logits = jnp.dot(inputs, router_weight, preferred_element_type=jnp.float32)
    logits = lax.psum(partial_logits, "dp")
    labels = jnp.arange(experts, dtype=jnp.int32)
    first_hot = (expert_ids[:, 0:1] == labels[None, :]).astype(jnp.float32)
    second_hot = (expert_ids[:, 1:2] == labels[None, :]).astype(jnp.float32)
    logit_gap = jnp.sum(logits * (first_hot - second_hot), axis=1)
    pick_gates = jnp.concatenate([jax.nn.sigmoid(logit_gap), jax.nn.sigmoid(-logit_gap)]).astype(
        jnp.bfloat16
    )
    pick_ids = jnp.concatenate([expert_ids[:, 0], expert_ids[:, 1]])
    position = jnp.arange(2 * per_group, dtype=jnp.int32) % per_group
    is_live = position < live_counts[0]
    one_hot = ((pick_ids[:, None] == labels[None, :]) & is_live[:, None]).astype(jnp.int32)
    pick_rank = jnp.sum(jnp.cumsum(one_hot, axis=0) * one_hot, axis=1) - 1
    overflow = experts * capacity
    pick_slot = jnp.where(is_live, pick_ids * capacity + pick_rank, overflow)
    slot_pick = (
        jnp.full((overflow,), 2 * per_group, jnp.int32)
        .at[pick_slot]
        .set(jnp.arange(2 * per_group, dtype=jnp.int32), mode="drop")
    )
    target = jnp.arange(groups * capacity, dtype=jnp.int32)
    expert_slot = target // capacity // column_parts * capacity + target % capacity
    send_pick = jnp.take(slot_pick, expert_slot, axis=0)
    send_token = jnp.where(send_pick < 2 * per_group, send_pick % per_group, per_group)
    send_rows = jnp.take(inputs, send_token, axis=0, mode="fill", fill_value=0)
    send_grad = jnp.take(grad_out, send_token, axis=0, mode="fill", fill_value=0)
    send_gate = jnp.take(pick_gates, send_pick, axis=0, mode="fill", fill_value=0)
    rows_in, rows_grad, gate_in = (
        lax.all_to_all(send_rows, "expert", split_axis=0, concat_axis=0, tiled=True),
        lax.all_to_all(send_grad, "expert", split_axis=0, concat_axis=0, tiled=True),
        lax.all_to_all(send_gate, "expert", split_axis=0, concat_axis=0, tiled=True),
    )
    before_part = jnp.dot(rows_in, up_weight, preferred_element_type=jnp.float32)
    back_part = jnp.dot(rows_grad, down_weight, preferred_element_type=jnp.float32)
    gate_column = gate_in.astype(jnp.float32)[:, None]
    before_act, back_act = (
        lax.psum(before_part.astype(jnp.bfloat16), "dp").astype(jnp.float32),
        lax.psum(back_part.astype(jnp.bfloat16), "dp").astype(jnp.float32),
    )
    gate_part, inner_grad, weighted = activate(before_act, back_act, gate_column)
    contract_rows = (((0,), (0,)), ((), ()))
    grad_up = lax.dot_general(
        rows_in, inner_grad, contract_rows, preferred_element_type=jnp.float32
    ).astype(jnp.bfloat16)
    grad_down = lax.dot_general(
        rows_grad, weighted, contract_rows, preferred_element_type=jnp.float32
    ).astype(jnp.bfloat16)
    contract_units = (((1,), (1,)), ((), ()))
    input_part = lax.dot_general(
        inner_grad, up_weight, contract_units, preferred_element_type=jnp.float32
    ).astype(jnp.bfloat16)
    back_rows, back_gate = (
        lax.all_to_all(input_part, "expert", split_axis=0, concat_axis=0, tiled=True),
        lax.all_to_all(
            gate_part.astype(jnp.bfloat16), "expert", split_axis=0, concat_axis=0, tiled=True
        ),
    )
    summed_rows = jnp.sum(
        back_rows.astype(jnp.float32).reshape(experts, column_parts, capacity, share), axis=1
    ).reshape(overflow, share)
    summed_gate = jnp.sum(
        back_gate.astype(jnp.float32).reshape(experts, column_parts, capacity), axis=1
    ).reshape(overflow)
    part_pick = jnp.take(summed_rows, pick_slot, axis=0, mode="fill", fill_value=0)
    gate_pick = jnp.take(summed_gate, pick_slot, axis=0, mode="fill", fill_value=0)
    gate_value = pick_gates.astype(jnp.float32)
    delta = lax.optimization_barrier(
        (gate_pick * gate_value * (1.0 - gate_value)).astype(jnp.bfloat16)
    ).astype(jnp.float32)
    delta_diff = delta[:per_group] - delta[per_group:]
    logit_grad = delta_diff[:, None] * (first_hot - second_hot)
    router_side = jnp.dot(
        logit_grad, router_weight.astype(jnp.float32).T, precision=lax.Precision.HIGHEST
    )
    grad_inputs = (
        grad_out.astype(jnp.float32) + (part_pick[:per_group] + part_pick[per_group:]) + router_side
    ).astype(jnp.bfloat16)
    router_term = jnp.dot(inputs.astype(jnp.float32).T, logit_grad, precision=lax.Precision.HIGHEST)
    grad_router = lax.psum(router_term, "expert")
    return (grad_inputs, grad_up, grad_down, grad_router)


def solution(mesh):
    placed = (
        P("expert", "dp"),
        P("expert", "dp"),
        P("expert", None),
        P("expert"),
        P("dp", None),
        P("dp", "expert"),
        P("dp", "expert"),
    )
    return jax.shard_map(
        local,
        mesh=mesh,
        in_specs=placed,
        out_specs=(P("expert", "dp"), P("dp", "expert"), P("dp", "expert"), P("dp", None)),
        check_vma=False,
    )
```

profile of v0, /device:TPU:1, one launch (start us, length us, event | category | flops | bytes accessed | tf_op | source)
XLA Modules:
  0.0 425.7 jit_solution(18165804764282503032)
XLA Ops:
  7.2 0.0 copy-start
  7.2 0.0 copy-start.2
  7.2 0.8 slice_bitcast_fusion.1
  8.6 0.1 pad_add_fusion
  8.7 0.1 fusion.17
  8.8 0.2 reduce_window_sum.11
  9.0 0.2 select_reduce_fusion
  9.2 0.1 fusion.52
  9.3 1.0 scatter_custom_fusion
  10.3 6.6 %gather_fusion = s32[1024]{0:T(1024)S(1)} fusion(s32[128]{0:T(128)S(1)} %scatter_custom_fusion, s32[1024]{0:T(1024)S(1)} %broadcast_clamp_fusion.2), kind=kCustom, calls=%fused_computation.2 | custom fusion | bytes 12288 | tf_op jit(solution)/shard_map/jit(_take)/gather | solution.py:60
  16.8 0.0 copy-start.1
  16.9 0.0 copy-done.2
  16.9 3.9 gather_fusion.4
  20.8 0.0 copy-done.1
  20.8 3.9 gather_fusion.5
  24.8 1.2 broadcast_select_fusion
  25.9 61.2 %all_to_all.45 = bf16[32,32,384]{2,1,0:T(8,128)(2,1)S(1)} all-to-all(bf16[32,32,384]{2,1,0:T(8,128)(2,1)S(1)} %bitcast.49), channel_id=1, replica_groups=mesh['dp'=16,'expert'=32] {'expert'}, dimensions={0} | all-to-all | bytes 1572864 | tf_op jit(solution)/shard_map/all_to_all | solution.py:66
  87.1 0.0 copy-start.6
  87.1 4.1 all-to-all-start.1
  91.2 0.0 all-reduce.3.cloned.1.call-start
  91.2 0.0 copy-done
  91.3 2.5 convolution_convert_fusion
  93.8 0.0 copy-start.9
  93.8 42.0 %all-to-all-done.1 = bf16[32,32,384]{2,1,0:T(8,128)(2,1)S(1)} async-done(((bf16[32,32,384]{2,1,0:T(8,128)(2,1)}), bf16[32,32,384]{2,1,0:T(8,128)(2,1)S(1)}, u32[]{:S(2)}, u32[]{:S(2)}) %all-to-all-start.1) | async-done | bytes 786464 | tf_op jit(solution)/shard_map/all_to_all | solution.py:67
  135.8 4.0 convolution_convert_fusion.1
  139.8 0.0 copy-done.6
  139.8 0.0 all-reduce.3.cloned.1.call-update
  139.9 0.0 copy-done.9
  139.9 0.1 fusion.58
  140.0 34.2 %psum.28 = f32[64,4]{0,1:T(4,128)S(1)} all-reduce(f32[64,4]{0,1:T(4,128)S(1)} %fusion.58), channel_id=1, replica_groups=mesh['dp'=16,'expert'=32] {'dp'}, use_global_device_ids=true, to_apply=%region_3.4 | all-reduce | flops 256 | bytes 2048 | tf_op jit(solution)/shard_map/psum | solution.py:38
  174.3 91.7 %all-reduce.3.cloned.1.call-done = (bf16[1024,1024]{1,0:T(8,128)(2,1)}, bf16[1024,1024]{1,0:T(8,128)(2,1)}) async-done(((bf16[1024,1024]{1,0:T(8,128)(2,1)}, bf16[1024,1024]{1,0:T(8,128)(2,1)}), (bf16[1024,1024]{1,0:T(8,128)(2,1)}, bf16[1024,1024]{1,0:T(8,128)(2,1)})) %all-reduce.3.cloned.1.call-update) | async-done | bytes 4194320 | tf_op jit(solution)/shard_map/psum | solution.py:75
  265.9 0.0 copy-done.7
  265.9 3.8 fusion.9
  269.7 0.0 copy-done.5
  269.7 0.6 fusion.2
  270.3 0.7 convert_element_type.131
  271.0 13.2 %all-to-all-start.4 = ((bf16[32,32,1]{1,2,0:T(2,128)(2,1)}), bf16[32,32,1]{1,2,0:T(2,128)(2,1)S(1)}, u32[]{:S(2)}, u32[]{:S(2)}) async-start(bf16[32,32,1]{1,2,0:T(2,128)(2,1)} %convert_element_type.131), calls=%async_computation.4 | async-start | bytes 32768 | tf_op jit(solution)/shard_map/all_to_all | solution.py:91
  284.2 0.1 gather.26
  284.3 11.6 %all-to-all-done.4 = bf16[32,32,1]{1,2,0:T(2,128)(2,1)S(1)} async-done(((bf16[32,32,1]{1,2,0:T(2,128)(2,1)}), bf16[32,32,1]{1,2,0:T(2,128)(2,1)S(1)}, u32[]{:S(2)}, u32[]{:S(2)}) %all-to-all-start.4) | async-done | bytes 2080 | tf_op jit(solution)/shard_map/all_to_all | solution.py:91
  296.0 0.1 reshape.485
  296.0 1.2 gather_fusion.3
  297.3 0.1 multiply_convert_fusion.4
  297.4 6.5 %gather_fusion.1 = bf16[1024]{0:T(1024)(128)(2,1)S(1)} fusion(bf16[128]{0:T(256)(128)(2,1)S(1)} %get-tuple-element.9, s32[1024]{0:T(1024)S(1)} %broadcast_clamp_fusion.1), kind=kCustom, calls=%fused_computation.3 | custom fusion | bytes 8192 | tf_op jit(solution)/shard_map/jit(_take)/gather | solution.py:64
  303.9 0.1 gather.29
  304.0 15.4 %all_to_all.46 = bf16[32,32,1]{1,2,0:T(2,128)(2,1)S(1)} all-to-all(bf16[32,32,1]{1,2,0:T(2,128)(2,1)S(1)} %copy.11), channel_id=1, replica_groups=mesh['dp'=16,'expert'=32] {'expert'}, dimensions={0} | all-to-all | bytes 4096 | tf_op jit(solution)/shard_map/all_to_all | solution.py:68
  319.4 0.1 convert_reduce_fusion.2
  319.5 0.1 reshape.486
  319.6 0.0 copy-done.3
  319.6 4.1 fusion.1
  323.7 0.0 copy-start.4
  323.7 2.2 convolution_convert_fusion.3
  325.8 0.0 copy-done.4
  325.8 5.1 %all-to-all-start.3 = ((bf16[32,32,384]{2,1,0:T(8,128)(2,1)}), bf16[32,32,384]{2,1,0:T(8,128)(2,1)}, u32[]{:S(2)}, u32[]{:S(2)}) async-start(bf16[32,32,384]{2,1,0:T(8,128)(2,1)} %bitcast.50), calls=%async_computation.3 | async-start | bytes 1572864 | tf_op jit(solution)/shard_map/all_to_all | solution.py:90
  330.9 0.1 slice_subtract_fusion
  331.0 0.1 convolution_bitcast_fusion
  331.1 76.7 %psum.31 = f32[384,4]{0,1:T(4,128)} all-reduce(f32[384,4]{0,1:T(4,128)S(1)} %convolution_bitcast_fusion), channel_id=1, replica_groups=mesh['dp'=16,'expert'=32] {'expert'}, use_global_device_ids=true, to_apply=%region_10.12 | all-reduce | flops 1536 | bytes 12288 | tf_op jit(solution)/shard_map/psum | solution.py:116
  407.9 3.8 convolution_convert_fusion.2
  411.6 0.0 copy-done.8
  411.7 4.2 fusion.13
  415.8 0.0 all-to-all-done.3
  415.8 1.3 convert_reduce_fusion
  417.1 0.8 gather_fusion.2
  417.9 0.1 broadcast_select_fusion.2
  418.0 0.9 fusion.14
  (19 shorter events, 0.2 us)
Async XLA Ops:
  7.2 84.1 %copy-start = (bf16[384,1024]{1,0:T(8,128)(2,1)S(1)}, bf16[384,1024]{1,0:T(8,128)(2,1)}, u32[]{:S(2)}) copy-start(bf16[384,1024]{1,0:T(8,128)(2,1)} %param.14) | copy-start | bytes 2359300
  7.2 9.7 %copy-start.2 = (bf16[64,384]{1,0:T(8,128)(2,1)S(1)}, bf16[64,384]{1,0:T(8,128)(2,1)}, u32[]{:S(2)}) copy-start(bf16[64,384]{1,0:T(8,128)(2,1)} %param.10) | copy-start | bytes 147460
  16.8 4.0 copy-start.1
  87.1 52.7 %copy-start.6 = (bf16[32,32,384]{2,1,0:T(8,128)(2,1)}, bf16[32,32,384]{2,1,0:T(8,128)(2,1)S(1)}, u32[]{:S(2)}) copy-start(bf16[32,32,384]{2,1,0:T(8,128)(2,1)S(1)} %all_to_all.45) | copy-start | bytes 2359300
  87.1 48.7 %all-to-all-start.1 = ((bf16[32,32,384]{2,1,0:T(8,128)(2,1)}), bf16[32,32,384]{2,1,0:T(8,128)(2,1)S(1)}, u32[]{:S(2)}, u32[]{:S(2)}) async-start(bf16[32,32,384]{2,1,0:T(8,128)(2,1)} %bitcast.8), calls=%async_computation.1 | async-start | bytes 1572864 | tf_op jit(solution)/shard_map/all_to_all | solution.py:67
  91.2 174.7 %all-reduce.3.cloned.1.call-start = ((), (), s32[]{:S(2)}) async-start(), calls=%async_computation.5 | async-start | bytes 8388608 | tf_op jit(solution)/shard_map/psum | solution.py:75
  93.8 46.1 %copy-start.9 = (bf16[384,4]{0,1:T(4,128)(2,1)S(1)}, bf16[384,4]{0,1:T(4,128)(2,1)}, u32[]{:S(2)}) copy-start(bf16[384,4]{0,1:T(4,128)(2,1)} %param.13) | copy-start | bytes 9220
  135.8 130.1 %copy-start.7 = (bf16[32,32,384]{2,1,0:T(8,128)(2,1)}, bf16[32,32,384]{2,1,0:T(8,128)(2,1)S(1)}, u32[]{:S(2)}) copy-start(bf16[32,32,384]{2,1,0:T(8,128)(2,1)S(1)} %all-to-all-done.1) | copy-start | bytes 2359300
  265.9 3.8 copy-start.5
  269.7 49.8 %copy-start.3 = (bf16[1024,1024]{1,0:T(8,128)(2,1)S(1)}, bf16[1024,1024]{1,0:T(8,128)(2,1)}, u32[]{:S(2)}) copy-start(bf16[1024,1024]{1,0:T(8,128)(2,1)} %get-tuple-element.6) | copy-start | bytes 6291460
  271.0 24.9 %all-to-all-start.4 = ((bf16[32,32,1]{1,2,0:T(2,128)(2,1)}), bf16[32,32,1]{1,2,0:T(2,128)(2,1)S(1)}, u32[]{:S(2)}, u32[]{:S(2)}) async-start(bf16[32,32,1]{1,2,0:T(2,128)(2,1)} %convert_element_type.131), calls=%async_computation.4 | async-start | bytes 32768 | tf_op jit(solution)/shard_map/all_to_all | solution.py:91
  323.7 2.2 copy-start.4
  325.8 90.0 %all-to-all-start.3 = ((bf16[32,32,384]{2,1,0:T(8,128)(2,1)}), bf16[32,32,384]{2,1,0:T(8,128)(2,1)}, u32[]{:S(2)}, u32[]{:S(2)}) async-start(bf16[32,32,384]{2,1,0:T(8,128)(2,1)} %bitcast.50), calls=%async_computation.3 | async-start | bytes 1572864 | tf_op jit(solution)/shard_map/all_to_all | solution.py:90
  407.9 3.8 copy-start.8
Sparse Core Ops, SparseCore 0:
  140.0 125.8 all-reduce.2
where the time goes:
time: 426 us
  blocking collectives  188 us (44%)
  waiting for transfers between devices  145 us (34%)
  local copies, waits for them, and re-layouts  25.7 us (6%)
  starting transfers between devices  22.4 us (5%)
  matrix products  17.8 us (4%)
  between operations  14.9 us (3%)
  other arithmetic  12 us (3%)
    psum x1, waiting for transfers between devices, local(): lax.psum(back_part.astype(jnp.bfloat16), 'dp').astype(jnp.float32)  91.7 us
    psum x1, blocking collectives, local(): grad_router = lax.psum(router_term, 'expert')  76.7 us
    all_to_all x1, blocking collectives, local(): lax.all_to_all(send_rows, 'expert', split_axis=0, concat_axis=0, tiled=True)  61.2 us
    all_to_all x1, waiting for transfers between devices, local(): lax.all_to_all(send_grad, 'expert', split_axis=0, concat_axis=0, tiled=True)  42 us
    psum x1, blocking collectives, local(): logits = lax.psum(partial_logits, 'dp')  34.2 us
    all_to_all x1, blocking collectives, local(): lax.all_to_all(send_gate, 'expert', split_axis=0, concat_axis=0, tiled=True)  15.4 us
    all_to_all x1, starting transfers between devices, local(): lax.all_to_all(gate_part.astype(jnp.bfloat16), 'expert', split_axis=0, co...  13.2 us
    all_to_all x1, waiting for transfers between devices, local(): lax.all_to_all(gate_part.astype(jnp.bfloat16), 'expert', split_axis=0, co...  11.6 us
  transfers between devices with their start and end apart: 4, of which 3 were waited for; matrix products, arithmetic and copies ran while one was open for 3% of the time, Pallas kernels for 0%

commit v1 on v0

--- a/solution.py
+++ b/solution.py
@@ -72,7 +72,7 @@
     gate_column = gate_in.astype(jnp.float32)[:, None]
     before_act, back_act = (
         lax.psum(before_part.astype(jnp.bfloat16), "dp").astype(jnp.float32),
-        lax.psum(back_part.astype(jnp.bfloat16), "dp").astype(jnp.float32),
+        jnp.sum(lax.all_gather(back_part.astype(jnp.bfloat16), "dp"), axis=0).astype(jnp.float32),
     )
     gate_part, inner_grad, weighted = activate(before_act, back_act, gate_column)
     contract_rows = (((0,), (0,)), ((), ()))

time: 426 us -> 605 us (1.42)
  waiting for transfers between devices: 145 us -> 308 us
  other arithmetic: 12 us -> 28 us
    all_gather x0 -> x1, waiting for transfers between devices: none -> 212 us  [local(): lax.all_gather(back_part.astype(jnp.bfloat16), 'dp')]
    psum x1, waiting for transfers between devices: 91.7 us -> 42.7 us  [local(): lax.psum(before_part.astype(jnp.bfloat16), 'dp').astype(jnp.float32)]
    reduce_sum x0 -> x1, other arithmetic: none -> 13 us  [local(): jnp.sum(lax.all_gather(back_part.astype(jnp.bfloat16), 'dp'), axis=0)]
  transfers between devices with their start and end apart: 4 -> 5, of which waited for: 3 -> 4; matrix products, arithmetic and copies ran while one was open for 3% -> 3% of each run, Pallas kernels for 0% -> 0%
where the time goes in v1:
time: 605 us; the launch traced here: 604 us
  waiting for transfers between devices  308 us (51%)
  blocking collectives  187 us (31%)
  other arithmetic  28 us (5%)
  local copies, waits for them, and re-layouts  25.7 us (4%)
  starting transfers between devices  22.3 us (4%)
  matrix products  17.8 us (3%)
  between operations  14.9 us (2%)
    all_gather x1, waiting for transfers between devices, local(): lax.all_gather(back_part.astype(jnp.bfloat16), 'dp')  212 us
    psum x1, blocking collectives, local(): grad_router = lax.psum(router_term, 'expert')  76.7 us
    all_to_all x1, blocking collectives, local(): lax.all_to_all(send_rows, 'expert', split_axis=0, concat_axis=0, tiled=True)  61.2 us
    psum x1, waiting for transfers between devices, local(): lax.psum(before_part.astype(jnp.bfloat16), 'dp').astype(jnp.float32)  42.7 us
    all_to_all x1, waiting for transfers between devices, local(): lax.all_to_all(send_grad, 'expert', split_axis=0, concat_axis=0, tiled=True)  41.9 us
    psum x1, blocking collectives, local(): logits = lax.psum(partial_logits, 'dp')  33.4 us
    all_to_all x1, blocking collectives, local(): lax.all_to_all(send_gate, 'expert', split_axis=0, concat_axis=0, tiled=True)  15.4 us
    reduce_sum x1, other arithmetic, local(): jnp.sum(lax.all_gather(back_part.astype(jnp.bfloat16), 'dp'), axis=0)  13 us
  transfers between devices with their start and end apart: 5, of which 4 were waited for; matrix products, arithmetic and copies ran while one was open for 3% of the time, Pallas kernels for 0%

profile of v1, /device:TPU:1, one launch (start us, length us, event | category | flops | bytes accessed | tf_op | source)
XLA Modules:
  0.0 603.9 jit_solution(4947627519335721398)
XLA Ops:
  7.2 0.0 copy-start
  7.2 0.0 copy-start.1
  7.2 0.8 slice_bitcast_fusion.1
  8.6 0.1 pad_add_fusion
  8.7 0.1 fusion.17
  8.8 0.2 reduce_window_sum.11
  9.0 0.2 select_reduce_fusion
  9.2 0.1 fusion.52
  9.3 1.0 scatter_custom_fusion
  10.3 6.6 %gather_fusion = s32[1024]{0:T(1024)S(1)} fusion(s32[128]{0:T(128)S(1)} %scatter_custom_fusion, s32[1024]{0:T(1024)S(1)} %broadcast_clamp_fusion.2), kind=kCustom, calls=%fused_computation.2 | custom fusion | bytes 12288 | tf_op jit(solution)/shard_map/jit(_take)/gather | solution.py:60
  16.8 0.0 copy-start.2
  16.9 0.0 copy-done.1
  16.9 3.9 gather_fusion.5
  20.8 0.0 copy-done.2
  20.8 3.9 gather_fusion.4
  24.8 1.2 broadcast_select_fusion
  25.9 61.2 %all_to_all.45 = bf16[32,32,384]{2,1,0:T(8,128)(2,1)S(1)} all-to-all(bf16[32,32,384]{2,1,0:T(8,128)(2,1)S(1)} %bitcast.51), channel_id=1, replica_groups=mesh['dp'=16,'expert'=32] {'expert'}, dimensions={0} | all-to-all | bytes 1572864 | tf_op jit(solution)/shard_map/all_to_all | solution.py:66
  87.1 4.1 all-to-all-start.1
  91.2 0.0 all-reduce.2.cloned.1.call-start
  91.2 0.0 copy-done
  91.3 2.6 convolution_convert_fusion
  93.8 0.0 all-reduce.2.cloned.1.call-update
  93.8 0.0 all-gather.3.cloned.1.call-start
  93.9 41.9 %all-to-all-done.1 = bf16[32,32,384]{2,1,0:T(8,128)(2,1)S(1)} async-done(((bf16[32,32,384]{2,1,0:T(8,128)(2,1)}), bf16[32,32,384]{2,1,0:T(8,128)(2,1)S(1)}, u32[]{:S(2)}, u32[]{:S(2)}) %all-to-all-start.1) | async-done | bytes 786464 | tf_op jit(solution)/shard_map/all_to_all | solution.py:67
  135.8 4.0 convolution_convert_fusion.1
  139.8 0.0 copy-done.5
  139.8 0.0 all-gather.3.cloned.1.call-update
  139.8 0.0 copy-done.8
  139.8 0.1 fusion.58
  140.0 33.4 %psum.21 = f32[64,4]{0,1:T(4,128)S(1)} all-reduce(f32[64,4]{0,1:T(4,128)S(1)} %fusion.58), channel_id=1, replica_groups=mesh['dp'=16,'expert'=32] {'dp'}, use_global_device_ids=true, to_apply=%region_3.4 | all-reduce | flops 256 | bytes 2048 | tf_op jit(solution)/shard_map/psum | solution.py:38
  173.5 42.7 %all-reduce.2.cloned.1.call-done = bf16[1024,1024]{1,0:T(8,128)(2,1)} async-done(((bf16[1024,1024]{1,0:T(8,128)(2,1)}), bf16[1024,1024]{1,0:T(8,128)(2,1)}) %all-reduce.2.cloned.1.call-update) | async-done | bytes 2097168 | tf_op jit(solution)/shard_map/psum | solution.py:74
  216.2 4.4 fusion.9
  220.5 0.0 copy-done.6
  220.5 212.1 %all-gather.3.cloned.1.call-done = bf16[16384,1024]{1,0:T(8,128)(2,1)} async-done(((bf16[1024,1024]{1,0:T(8,128)(2,1)}), bf16[16384,1024]{1,0:T(8,128)(2,1)}) %all-gather.3.cloned.1.call-update) | async-done | bytes 33554448 | tf_op jit(solution)/shard_map/all_gather | solution.py:75
  432.6 13.0 %reduce_sum.59 = bf16[1024,1024]{1,0:T(8,128)(2,1)} reduce(bf16[16,1024,1024]{2,1,0:T(8,128)(2,1)} %bitcast.45, bf16[]{:T(256)} %constant.167.clone.1), dimensions={0}, to_apply=%region_5.7 | reduce | flops 15728640 | bytes 35651584 | tf_op jit(solution)/shard_map/reduce_sum | solution.py:75
  445.7 3.0 fusion.2
  448.7 0.7 convert_element_type.133
  449.4 13.0 %all-to-all-start.4 = ((bf16[32,32,1]{1,2,0:T(2,128)(2,1)}), bf16[32,32,1]{1,2,0:T(2,128)(2,1)S(1)}, u32[]{:S(2)}, u32[]{:S(2)}) async-start(bf16[32,32,1]{1,2,0:T(2,128)(2,1)} %convert_element_type.133), calls=%async_computation.4 | async-start | bytes 32768 | tf_op jit(solution)/shard_map/all_to_all | solution.py:91
  462.4 0.1 gather.26
  462.5 11.6 %all-to-all-done.4 = bf16[32,32,1]{1,2,0:T(2,128)(2,1)S(1)} async-done(((bf16[32,32,1]{1,2,0:T(2,128)(2,1)}), bf16[32,32,1]{1,2,0:T(2,128)(2,1)S(1)}, u32[]{:S(2)}, u32[]{:S(2)}) %all-to-all-start.4) | async-done | bytes 2080 | tf_op jit(solution)/shard_map/all_to_all | solution.py:91
  474.1 0.1 reshape.485
  474.2 1.2 gather_fusion.3
  475.4 0.1 multiply_convert_fusion.4
  475.5 6.5 %gather_fusion.1 = bf16[1024]{0:T(1024)(128)(2,1)S(1)} fusion(bf16[128]{0:T(256)(128)(2,1)S(1)} %get-tuple-element.7, s32[1024]{0:T(1024)S(1)} %broadcast_clamp_fusion.1), kind=kCustom, calls=%fused_computation.3 | custom fusion | bytes 8192 | tf_op jit(solution)/shard_map/jit(_take)/gather | solution.py:64
  482.0 0.1 gather.29
  482.2 15.4 %all_to_all.46 = bf16[32,32,1]{1,2,0:T(2,128)(2,1)S(1)} all-to-all(bf16[32,32,1]{1,2,0:T(2,128)(2,1)S(1)} %copy.11), channel_id=1, replica_groups=mesh['dp'=16,'expert'=32] {'expert'}, dimensions={0} | all-to-all | bytes 4096 | tf_op jit(solution)/shard_map/all_to_all | solution.py:68
  497.6 0.1 convert_reduce_fusion.2
  497.6 0.1 reshape.486
  497.7 0.0 copy-done.3
  497.7 4.1 fusion.1
  501.8 0.0 copy-start.4
  501.8 2.2 convolution_convert_fusion.3
  504.0 0.0 copy-done.4
  504.0 5.1 all-to-all-start.3
  509.1 0.1 slice_subtract_fusion
  509.2 0.1 convolution_bitcast_fusion
  509.3 76.7 %psum.23 = f32[384,4]{0,1:T(4,128)} all-reduce(f32[384,4]{0,1:T(4,128)S(1)} %convolution_bitcast_fusion), channel_id=1, replica_groups=mesh['dp'=16,'expert'=32] {'expert'}, use_global_device_ids=true, to_apply=%region_10.12 | all-reduce | flops 1536 | bytes 12288 | tf_op jit(solution)/shard_map/psum | solution.py:116
  586.1 3.8 convolution_convert_fusion.2
  589.9 4.2 fusion.13
  594.0 0.0 all-to-all-done.3
  594.0 1.3 convert_reduce_fusion
  595.3 0.8 gather_fusion.2
  596.1 0.1 broadcast_select_fusion.2
  596.2 0.9 fusion.14
  (21 shorter events, 0.2 us)
Async XLA Ops:
  7.2 84.1 %copy-start = (bf16[384,1024]{1,0:T(8,128)(2,1)S(1)}, bf16[384,1024]{1,0:T(8,128)(2,1)}, u32[]{:S(2)}) copy-start(bf16[384,1024]{1,0:T(8,128)(2,1)} %param.14) | copy-start | bytes 2359300
  7.2 9.7 %copy-start.1 = (bf16[64,384]{1,0:T(8,128)(2,1)S(1)}, bf16[64,384]{1,0:T(8,128)(2,1)}, u32[]{:S(2)}) copy-start(bf16[64,384]{1,0:T(8,128)(2,1)} %param.9) | copy-start | bytes 147460
  16.8 4.0 copy-start.2
  87.1 52.7 %copy-start.5 = (bf16[32,32,384]{2,1,0:T(8,128)(2,1)}, bf16[32,32,384]{2,1,0:T(8,128)(2,1)S(1)}, u32[]{:S(2)}) copy-start(bf16[32,32,384]{2,1,0:T(8,128)(2,1)S(1)} %all_to_all.45) | copy-start | bytes 2359300
  87.1 48.7 %all-to-all-start.1 = ((bf16[32,32,384]{2,1,0:T(8,128)(2,1)}), bf16[32,32,384]{2,1,0:T(8,128)(2,1)S(1)}, u32[]{:S(2)}, u32[]{:S(2)}) async-start(bf16[32,32,384]{2,1,0:T(8,128)(2,1)} %bitcast.8), calls=%async_computation.1 | async-start | bytes 1572864 | tf_op jit(solution)/shard_map/all_to_all | solution.py:67
  91.2 125.0 %all-reduce.2.cloned.1.call-start = ((), (), s32[]{:S(2)}) async-start(), calls=%async_computation.5 | async-start | bytes 4194304 | tf_op jit(solution)/shard_map/psum | solution.py:74
  93.8 46.0 %copy-start.8 = (bf16[384,4]{0,1:T(4,128)(2,1)S(1)}, bf16[384,4]{0,1:T(4,128)(2,1)}, u32[]{:S(2)}) copy-start(bf16[384,4]{0,1:T(4,128)(2,1)} %param.13) | copy-start | bytes 9220
  93.8 338.8 %all-gather.3.cloned.1.call-start = ((), (), s32[]{:S(2)}) async-start(), calls=%async_computation.6 | async-start | bytes 35651584 | tf_op jit(solution)/shard_map/all_gather | solution.py:75
  135.8 84.7 %copy-start.6 = (bf16[32,32,384]{2,1,0:T(8,128)(2,1)}, bf16[32,32,384]{2,1,0:T(8,128)(2,1)S(1)}, u32[]{:S(2)}) copy-start(bf16[32,32,384]{2,1,0:T(8,128)(2,1)S(1)} %all-to-all-done.1) | copy-start | bytes 2359300
  445.7 52.0 %copy-start.3 = (bf16[1024,1024]{1,0:T(8,128)(2,1)S(1)}, bf16[1024,1024]{1,0:T(8,128)(2,1)}, u32[]{:S(2)}) copy-start(bf16[1024,1024]{1,0:T(8,128)(2,1)} %all-reduce.2.cloned.1.call-done) | copy-start | bytes 6291460
  449.4 24.7 %all-to-all-start.4 = ((bf16[32,32,1]{1,2,0:T(2,128)(2,1)}), bf16[32,32,1]{1,2,0:T(2,128)(2,1)S(1)}, u32[]{:S(2)}, u32[]{:S(2)}) async-start(bf16[32,32,1]{1,2,0:T(2,128)(2,1)} %convert_element_type.133), calls=%async_computation.4 | async-start | bytes 32768 | tf_op jit(solution)/shard_map/all_to_all | solution.py:91
  501.8 2.2 copy-start.4
  504.0 90.0 %all-to-all-start.3 = ((bf16[32,32,384]{2,1,0:T(8,128)(2,1)}), bf16[32,32,384]{2,1,0:T(8,128)(2,1)}, u32[]{:S(2)}, u32[]{:S(2)}) async-start(bf16[32,32,384]{2,1,0:T(8,128)(2,1)} %bitcast.52), calls=%async_computation.3 | async-start | bytes 1572864 | tf_op jit(solution)/shard_map/all_to_all | solution.py:90
  586.1 3.8 copy-start.7
Sparse Core Ops, SparseCore 0:
  95.3 120.7 all-reduce.1
  219.6 212.9 all-gather.2
